TPU v7x, 32 devices: a whole 2x2x4 slice. The times are simulated.
32 devices in a mesh: rep: 2 (over y), store: 4 (over z), tp: 4 (over x, core).
Axes of the slice: x: 2, y: 2, z: 4, core: 2. Of those that a mesh axis runs over, the one named last changes fastest.
Arguments:
- tokens: bfloat16 [384, 5120], P(('rep', 'store'), 'tp'), parts along dimension 0, may hold values from -6 to 6
- gate_weight: bfloat16 [5120, 16384], P('tp', 'store'), may hold values from -0.078125 to 0.078125
- up_weight: bfloat16 [5120, 16384], P('tp', 'store'), may hold values from -0.078125 to 0.078125
- down_weight: bfloat16 [16384, 5120], P('store', 'tp'), may hold values from -0.046875 to 0.046875
- factor_a: bfloat16 [128, 32, 5120], P(('rep', 'store'), None, 'tp'), parts along dimension 0, may hold values from -0.078125 to 0.078125
- factor_b: bfloat16 [128, 32, 16384], P(('rep', 'tp'), None, 'store'), parts along dimension 0, may hold values from -1.5 to 1.5
- adapter_slot: int32 [128], P('rep'), parts along dimension 0, may hold values from 0 to 63, as said below
- seg_adapter: int32 [8, 24], P(('rep', 'store')), parts along dimension 0, may hold values from 0 to 63, as said below
- row_segment: int32 [8, 48], P(('rep', 'store')), parts along dimension 0, may hold values from 0 to 23, never falling along the last dimension, each value on 1 to 4 neighbouring positions
Outputs:
- layer_out: bfloat16 [384, 5120], P(('rep', 'store'), 'tp'), parts along dimension 0
There are 2 independent parts, one for each index of `rep`. A program takes and returns all parts, laid end to end along the dimension named above; an argument that names none is the same for every part. Nothing has to cross between parts.
Inputs may be any that keep to these rules, and one draw needn't show every extreme that they name: A permutation: adapter a lies in row adapter_slot[a] of factor_a and factor_b; rows g * 16 up to (g + 1) * 16 belong to store index g. `seg_adapter`: the 24 segments of one store index name distinct adapters; at most 6 of them lie in the rows of one store index, and for every store index some store index holds exactly 6 of its segments' adapters.
All inputs are finite; a program needn't handle non-finite values.
Results may differ from a plain program's by a relative error of at most 0.02.
Values may be sent and summed in bfloat16 or wider, within the bound.
A program may use at most 128 MiB of HBM per device.

v0:
```python
import jax
import jax.numpy as jnp
from jax import lax
from jax.sharding import PartitionSpec as P


def lookup_table(table_vals, id_vals):
    hit_mask = id_vals[..., None] == jnp.arange(table_vals.shape[0], dtype=jnp.int32)
    return jnp.sum(jnp.where(hit_mask, table_vals, 0), axis=-1)


def body(
    tokens,
    gate_weight,
    up_weight,
    down_weight,
    factor_a,
    factor_b,
    adapter_slot,
    seg_adapter,
    row_segment,
):
    tok_dev = tokens.shape[0]
    d_loc = tokens.shape[1]
    ff_loc = gate_weight.shape[1]
    rank_both = factor_a.shape[1]
    rank_width = rank_both // 2
    adapter_rows = factor_a.shape[0]
    block_rows = factor_b.shape[0]
    nseg = seg_adapter.shape[1]
    store_count = lax.axis_size("store")
    store_index = lax.axis_index("store")
    tp_index = lax.axis_index("tp")
    total_rows = tok_dev * store_count
    seg_lists, row_lists = (
        lax.all_gather(seg_adapter, "store", axis=0, tiled=True),
        lax.all_gather(row_segment, "store", axis=0, tiled=True),
    )
    seg_rows = lookup_table(adapter_slot, seg_lists)
    seg_match = row_lists[..., None] == jnp.arange(nseg, dtype=jnp.int32)
    token_rows = jnp.sum(jnp.where(seg_match, seg_rows[:, None, :], 0), axis=-1).reshape(total_rows)
    piece_rows = lax.all_gather(tokens, "store", axis=0, tiled=True)
    projected = jnp.concatenate(
        [
            jnp.dot(piece_rows, gate_weight, preferred_element_type=jnp.float32),
            jnp.dot(piece_rows, up_weight, preferred_element_type=jnp.float32),
        ],
        axis=1,
    )
    capacity = max(2, nseg // store_count)
    owner_ids = seg_rows // adapter_rows
    local_ids = seg_rows % adapter_rows
    same_owner = owner_ids[:, :, None] == owner_ids[:, None, :]
    before = jnp.arange(nseg)[None, :] < jnp.arange(nseg)[:, None]
    rank_ids = jnp.sum(same_owner & before[None], axis=2)
    to_me = owner_ids == store_index
    wanted = to_me[:, :, None] & (rank_ids[:, :, None] == jnp.arange(capacity, dtype=jnp.int32))
    send_local = jnp.sum(jnp.where(wanted, local_ids[:, :, None], 0), axis=1)
    blocks = jnp.take(factor_a, send_local.reshape(-1), axis=0).reshape(
        store_count, capacity, rank_both, d_loc
    )
    received = lax.all_to_all(blocks, "store", split_axis=0, concat_axis=0, tiled=True)
    home_owner = lax.dynamic_index_in_dim(owner_ids, store_index, 0, keepdims=False)
    home_rank = lax.dynamic_index_in_dim(rank_ids, store_index, 0, keepdims=False)
    pick_index = home_owner * capacity + home_rank
    seg_blocks = jnp.take(
        received.reshape(store_count * capacity, rank_both, d_loc), pick_index, axis=0
    )
    scores = jnp.einsum("td,skd->tsk", tokens, seg_blocks, preferred_element_type=jnp.float32)
    local_mask = row_segment[0][:, None] == jnp.arange(nseg, dtype=jnp.int32)
    partial_value = jnp.sum(jnp.where(local_mask[:, :, None], scores, 0.0), axis=1)
    home_low = lax.psum(partial_value, "tp")
    low_rank = lax.all_gather(home_low, "store", axis=0, tiled=True)
    low_half = low_rank.astype(jnp.bfloat16)
    in_block = token_rows[:, None] == tp_index * block_rows + jnp.arange(
        block_rows, dtype=jnp.int32
    )

    def spread_rows(factor_half):
        placed = jnp.where(
            in_block[:, :, None], factor_half[:, None, :], jnp.zeros((), jnp.bfloat16)
        )
        return placed.reshape(total_rows, block_rows * rank_width)

    b_gate = factor_b[:, :rank_width, :].reshape(block_rows * rank_width, ff_loc)
    b_up = factor_b[:, rank_width:, :].reshape(block_rows * rank_width, ff_loc)
    gate_part = projected[:, :ff_loc] + jnp.dot(
        spread_rows(low_half[:, :rank_width]), b_gate, preferred_element_type=jnp.float32
    )
    up_part = projected[:, ff_loc:] + jnp.dot(
        spread_rows(low_half[:, rank_width:]), b_up, preferred_element_type=jnp.float32
    )
    gate_sum, up_sum = (
        lax.psum(gate_part.astype(jnp.bfloat16), "tp").astype(jnp.float32),
        lax.psum(up_part.astype(jnp.bfloat16), "tp").astype(jnp.float32),
    )
    hidden = (jax.nn.silu(gate_sum) * up_sum).astype(jnp.bfloat16)
    return lax.psum_scatter(
        jnp.dot(hidden, down_weight, preferred_element_type=jnp.float32).astype(jnp.bfloat16),
        "store",
        scatter_dimension=0,
        tiled=True,
    )


def solution(mesh):
    placed = (
        P(("rep", "store"), "tp"),
        P("tp", "store"),
        P("tp", "store"),
        P("store", "tp"),
        P(("rep", "store"), None, "tp"),
        P(("rep", "tp"), None, "store"),
        P("rep"),
        P(("rep", "store"), None),
        P(("rep", "store"), None),
    )
    return jax.shard_map(
        body, mesh=mesh, in_specs=placed, out_specs=P(("rep", "store"), "tp"), check_vma=False
    )
```

profile of v0, /device:TPU:0, one launch (start us, length us, event | category | flops | bytes accessed | tf_op | source)
XLA Modules:
  0.0 240.2 jit_solution(13401500088701037824)
XLA Ops:
  6.5 0.0 copy-start
  6.5 12.8 %all-gather.1 = s32[4,1,24]{2,1,0:T(1,128)S(1)} all-gather(s32[1,1,24]{2,1,0:T(1,128)} %bitcast.52), channel_id=1, replica_groups=mesh['rep'=2,'store'=4,'tp'=4] {'store'}, dimensions={0}, use_global_device_ids=true | all-gather | bytes 480 | tf_op jit(solution)/shard_map/all_gather | solution.py:36
  19.4 0.9 select_reduce_fusion.1
  20.3 0.2 convert_reduce_fusion
  20.5 0.2 select_reduce_fusion.2
  20.7 0.1 copy.12
  20.8 0.1 reshape.217
  20.9 0.1 copy.11
  21.0 0.0 copy-done
  21.0 0.7 gather_fusion
  21.7 1.6 broadcast_select_fusion
  23.3 0.0 copy-start.3
  23.3 0.0 copy-start.2
  23.3 0.0 slice-start
  23.3 4.6 %all-to-all-start = ((bf16[4,6,32,1280]{3,2,1,0:T(8,128)(2,1)}), bf16[4,6,32,1280]{3,2,1,0:T(8,128)(2,1)}, u32[]{:S(2)}, u32[]{:S(2)}) async-start(bf16[4,6,32,1280]{3,2,1,0:T(8,128)(2,1)} %broadcast_select_fusion), calls=%async_computation | async-start | bytes 3932160 | tf_op jit(solution)/shard_map/all_to_all | solution.py:62
  27.9 0.0 all-reduce.3.cloned.1.call-start
  27.9 0.0 copy-done.3
  27.9 35.8 %all-gather = s32[4,1,48]{2,1,0:T(1,128)S(1)} all-gather(s32[1,1,48]{2,1,0:T(1,128)S(1)} %bitcast.50), channel_id=1, replica_groups=mesh['rep'=2,'store'=4,'tp'=4] {'store'}, dimensions={0}, use_global_device_ids=true | all-gather | bytes 960 | tf_op jit(solution)/shard_map/all_gather | solution.py:37
  63.7 0.1 select_reduce_fusion
  63.8 0.1 eq.108
  64.0 0.0 copy-done.2
  64.0 23.8 %all_gather.12 = bf16[192,1280]{1,0:T(8,128)(2,1)S(1)} all-gather(bf16[48,1280]{1,0:T(8,128)(2,1)S(1)} %copy-done.2), channel_id=1, replica_groups=mesh['rep'=2,'store'=4,'tp'=4] {'store'}, dimensions={0}, use_global_device_ids=true | all-gather | bytes 614400 | tf_op jit(solution)/shard_map/all_gather | solution.py:42
  87.8 0.1 broadcast_compare_fusion
  87.9 0.0 slice-start.1
  87.9 0.0 slice-start.2
  87.9 8.0 %fusion.45 = f32[192,4096]{1,0:T(8,128)} fusion(bf16[192,1280]{1,0:T(8,128)(2,1)S(1)} %all_gather.12, bf16[1280,4096]{1,0:T(8,128)(2,1)} %param.11), kind=kOutput, calls=%fused_computation.74 | convolution fusion | flops 2013265920 | bytes 14123008 | tf_op jit(solution)/shard_map/dot_general | solution.py:46
  95.9 0.0 slice-done
  95.9 0.0 slice-done.1
  95.9 0.0 slice-done.2
  95.9 3.9 %fusion.44 = f32[192,4096]{1,0:T(8,128)} fusion(bf16[192,1280]{1,0:T(8,128)(2,1)S(1)} %all_gather.12, bf16[1280,4096]{1,0:T(8,128)(2,1)S(1)} %bitcast.45), kind=kOutput, calls=%fused_computation.73 | convolution fusion | flops 2013265920 | bytes 14123008 | tf_op jit(solution)/shard_map/dot_general | solution.py:45
  99.8 0.0 all-to-all-done
  99.8 2.2 gather_fusion.1
  102.0 0.7 fusion.22
  102.7 10.1 %psum.21 = bf16[48,32]{0,1:T(8,128)(2,1)S(1)} all-reduce(f32[48,32]{0,1:T(8,128)S(1)} %fusion.22), channel_id=1, replica_groups=mesh['rep'=2,'store'=4,'tp'=4] {'tp'}, use_global_device_ids=true, to_apply=%region_5.6 | all-reduce | flops 1536 | bytes 9216 | tf_op jit(solution)/shard_map/psum | solution.py:72
  112.9 13.1 %all-gather.2 = bf16[4,48,32]{1,2,0:T(8,128)(2,1)S(1)} all-gather(bf16[1,48,32]{1,2,0:T(8,128)(2,1)S(1)} %bitcast.47), channel_id=1, replica_groups=mesh['rep'=2,'store'=4,'tp'=4] {'store'}, dimensions={0}, use_global_device_ids=true | all-gather | bytes 15360 | tf_op jit(solution)/shard_map/all_gather | solution.py:73
  126.0 0.1 reshape.241
  126.1 0.0 copy-start.1
  126.1 0.0 copy-start.4
  126.1 4.4 %fusion.2 = bf16[192,4096]{1,0:T(8,128)(2,1)} fusion(f32[192,4096]{1,0:T(8,128)} %fusion.45, bf16[16,32,4096]{2,1,0:T(8,128)(2,1)} %param.14, pred[192,16]{0,1:T(8,128)(4,1)S(1)} %broadcast_compare_fusion, bf16[192,16]{0,1:T(8,128)(2,1)S(1)} %get-tuple-element.12), kind=kOutput, calls=%fused_computation.6 | convolution fusion | flops 404275200 | bytes 6824960 | tf_op jit(solution)/shard_map/dot_general | solution.py:90
  130.6 0.0 copy-done.1
  130.6 0.8 copy-done.4
  131.4 1.8 fusion.3
  133.2 0.0 all-reduce.3.cloned.1.call-update
  133.2 0.0 reduce-scatter.2.cloned.1.call-start
  133.2 70.1 %all-reduce.3.cloned.1.call-done = (bf16[192,4096]{1,0:T(8,128)(2,1)}, bf16[192,4096]{1,0:T(8,128)(2,1)}) async-done(((bf16[192,4096]{1,0:T(8,128)(2,1)}, bf16[192,4096]{1,0:T(8,128)(2,1)}), (bf16[192,4096]{1,0:T(8,128)(2,1)}, bf16[192,4096]{1,0:T(8,128)(2,1)})) %all-reduce.3.cloned.1.call-update) | async-done | bytes 3145744 | tf_op jit(solution)/shard_map/psum | solution.py:95
  203.3 8.5 %convolution_convert_fusion = bf16[192,1280]{1,0:T(8,128)(2,1)} fusion(bf16[4096,1280]{1,0:T(8,128)(2,1)} %param.12, bf16[192,4096]{1,0:T(8,128)(2,1)} %get-tuple-element.5, bf16[192,4096]{1,0:T(8,128)(2,1)} %get-tuple-element.6), kind=kOutput, calls=%fused_computation.15 | convolution fusion | flops 2019803136 | bytes 14123008 | tf_op jit(solution)/shard_map/dot_general | solution.py:99
  211.8 0.0 reduce-scatter.2.cloned.1.call-update
  211.8 21.6 %reduce-scatter.2.cloned.1.call-done = bf16[48,1280]{1,0:T(8,128)(2,1)} async-done(((bf16[192,1280]{1,0:T(8,128)(2,1)}), bf16[48,1280]{1,0:T(8,128)(2,1)}) %reduce-scatter.2.cloned.1.call-update) | async-done | bytes 122896 | tf_op jit(solution)/shard_map/reduce_scatter | solution.py:98
  (14 shorter events, 0.1 us)
Async XLA Ops:
  6.5 14.5 %copy-start = (bf16[16,32,1280]{2,1,0:T(8,128)(2,1)S(1)}, bf16[16,32,1280]{2,1,0:T(8,128)(2,1)}, u32[]{:S(2)}) copy-start(bf16[16,32,1280]{2,1,0:T(8,128)(2,1)} %param.13) | copy-start | bytes 3932164
  23.3 4.6 %copy-start.3 = (s32[1,48]{1,0:T(1,128)S(1)}, s32[1,48]{1,0:T(1,128)}, u32[]{:S(2)}) copy-start(s32[1,48]{1,0:T(1,128)} %param.17) | copy-start | bytes 580
  23.3 40.7 %copy-start.2 = (bf16[48,1280]{1,0:T(8,128)(2,1)S(1)}, bf16[48,1280]{1,0:T(8,128)(2,1)}, u32[]{:S(2)}) copy-start(bf16[48,1280]{1,0:T(8,128)(2,1)} %param.9) | copy-start | bytes 368644
  23.3 72.6 %slice-start = ((s8[10485760]{0:T(1024)(128)(4,1)}), s8[2097152]{0:T(1024)(128)(4,1)S(1)}, s32[]{:S(2)}) async-start(s8[10485760]{0:T(1024)(128)(4,1)} %bitcast.44), calls=%async_computation.4 | async-start | bytes 4194304
  23.3 76.5 %all-to-all-start = ((bf16[4,6,32,1280]{3,2,1,0:T(8,128)(2,1)}), bf16[4,6,32,1280]{3,2,1,0:T(8,128)(2,1)}, u32[]{:S(2)}, u32[]{:S(2)}) async-start(bf16[4,6,32,1280]{3,2,1,0:T(8,128)(2,1)} %broadcast_select_fusion), calls=%async_computation | async-start | bytes 3932160 | tf_op jit(solution)/shard_map/all_to_all | solution.py:62
  27.9 175.4 %all-reduce.3.cloned.1.call-start = ((), (), s32[]{:S(2)}) async-start(), calls=%async_computation.3 | async-start | bytes 6291456 | tf_op jit(solution)/shard_map/psum | solution.py:95
  87.9 8.0 %slice-start.1 = ((s8[10485760]{0:T(1024)(128)(4,1)}), s8[4194304]{0:T(1024)(128)(4,1)S(1)}, s32[]{:S(2)}) async-start(s8[10485760]{0:T(1024)(128)(4,1)} %bitcast.44), calls=%async_computation.5 | async-start | bytes 8388608
  87.9 8.0 %slice-start.2 = ((s8[10485760]{0:T(1024)(128)(4,1)}), s8[4194304]{0:T(1024)(128)(4,1)S(1)}, s32[]{:S(2)}) async-start(s8[10485760]{0:T(1024)(128)(4,1)} %bitcast.44), calls=%async_computation.6 | async-start | bytes 8388608
  126.1 4.5 %copy-start.1 = (f32[192,4096]{1,0:T(8,128)S(1)}, f32[192,4096]{1,0:T(8,128)}, u32[]{:S(2)}) copy-start(f32[192,4096]{1,0:T(8,128)} %fusion.44) | copy-start | bytes 9437188
  126.1 5.3 %copy-start.4 = (bf16[16,32,4096]{2,1,0:T(8,128)(2,1)S(1)}, bf16[16,32,4096]{2,1,0:T(8,128)(2,1)}, u32[]{:S(2)}) copy-start(bf16[16,32,4096]{2,1,0:T(8,128)(2,1)} %param.14) | copy-start | bytes 12582916
  133.2 100.2 %reduce-scatter.2.cloned.1.call-start = ((), (), s32[]{:S(2)}) async-start(), calls=%async_computation.2 | async-start | bytes 614400 | tf_op jit(solution)/shard_map/reduce_scatter | solution.py:98
Sparse Core Ops, SparseCore 0:
  133.3 69.9 all-reduce.2
  211.9 21.3 reduce-scatter.1
where the time goes:
time: 240 us
  blocking collectives  95.7 us (40%)
  waiting for transfers between devices  91.7 us (38%)
  matrix products  27.3 us (11%)
  between operations  13.6 us (6%)
  starting transfers between devices  4.65 us (2%)
  local copies, waits for them, and re-layouts  4.23 us (2%)
  other arithmetic  3.1 us (1%)
    psum x1, waiting for transfers between devices, body(): lax.psum(up_part.astype(jnp.bfloat16), 'tp').astype(jnp.float32)  70.1 us
    all_gather x1, blocking collectives, body(): lax.all_gather(row_segment, 'store', axis=0, tiled=True)  35.8 us
    all_gather x1, blocking collectives, body(): piece_rows = lax.all_gather(tokens, 'store', axis=0, tiled=True)  23.8 us
    reduce_scatter x1, waiting for transfers between devices, body(): lax.psum_scatter(jnp.dot(hidden, down_weight, preferred_element_type=jnp....  21.6 us
    all_gather x1, blocking collectives, body(): low_rank = lax.all_gather(home_low, 'store', axis=0, tiled=True)  13.1 us
    all_gather x1, blocking collectives, body(): lax.all_gather(seg_adapter, 'store', axis=0, tiled=True)  12.8 us
    psum x1, blocking collectives, body(): home_low = lax.psum(partial_value, 'tp')  10.1 us
    dot_general x1, matrix products, body(): jnp.dot(hidden, down_weight, preferred_element_type=jnp.float32)  8.46 us
  transfers between devices with their start and end apart: 3, of which 2 were waited for; matrix products, arithmetic and copies ran while one was open for 5% of the time, Pallas kernels for 0%

commit v1 on v0

--- a/solution.py
+++ b/solution.py
@@ -1,7 +1,17 @@
+import functools
 import jax
 import jax.numpy as jnp
 from jax import lax
+from jax.experimental import pallas as pl
+from jax.experimental.pallas import tpu as pltpu
 from jax.sharding import PartitionSpec as P
+
+MESH = pl.DeviceIdType.MESH
+CHUNK = 256
+SPLIT = (32, 16)
+LAGS = (1, 2, 3, 4)
+F32 = jnp.float32
+BF16 = jnp.bfloat16
 
 
 def lookup_table(table_vals, id_vals):
@@ -103,6 +113,362 @@
     )
 
 
+def dot(left, right, contract=(1, 0)):
+    dims = (((contract[0],), (contract[1],)), ((), ()))
+    return lax.dot_general(left, right, dims, preferred_element_type=F32)
+
+
+def fused_kernel(
+    tok_ref, gate_ref, up_ref, down_ref, fa_ref, fb_ref, slot_ref, seg_ref, row_ref,
+    out_ref,
+    meta, tok_a, tok_b, fa, w_buf, b_buf, d_buf,
+    low_send_a, low_send_b, low_recv_a, low_recv_b, spread_a, spread_b,
+    sib_send_a, sib_send_b, sib_recv_a, sib_recv_b, keep_a, keep_b,
+    x_send_a, x_send_b, x_recv_a, x_recv_b, hid_a, hid_b, acc_a, acc_b,
+    z_send_a, z_send_b, z_recv_a, z_recv_b,
+    load_w, load_b, load_d, load_fa,
+    meta_s, meta_r, tok_s, tok_r, low_s, low_r, sib_s, sib_r, x_s, x_r,
+    hx_s, hx_r, h1_s, h1_r, h3_s, h3_r, z_s, z_r,
+):
+    stores = lax.axis_size("store")
+    s = lax.axis_index("store")
+    t = lax.axis_index("tp")
+    core = lax.rem(t, 2)
+    sib = t + 1 - 2 * core
+    opp = lax.rem(t + 2, 4)
+    diag = lax.rem(sib + 2, 4)
+    rows_of = fa_ref.shape[0]
+    ff_loc, width = down_ref.shape
+    quarter = ff_loc // 4
+    w = CHUNK
+    chunks = quarter // w
+    toks, low_sends, low_recvs = (tok_a, tok_b), (low_send_a, low_send_b), (low_recv_a, low_recv_b)
+    spreads = (spread_a, spread_b)
+    sib_sends, sib_recvs, keeps = (sib_send_a, sib_send_b), (sib_recv_a, sib_recv_b), (keep_a, keep_b)
+    x_sends, x_recvs, hids, accs = (x_send_a, x_send_b), (x_recv_a, x_recv_b), (hid_a, hid_b), (acc_a, acc_b)
+    z_sends, z_recvs = (z_send_a, z_send_b), (z_recv_a, z_recv_b)
+    starts = (0, SPLIT[0])
+    pending = []
+
+    def remote(src, dst, send_sem, recv_sem, **where):
+        return pltpu.make_async_remote_copy(
+            src_ref=src, dst_ref=dst, send_sem=send_sem, recv_sem=recv_sem,
+            device_id=where, device_id_type=MESH,
+        )
+
+    load_a = pltpu.make_async_copy(fa_ref, fa, load_fa)
+    load_a.start()
+    owners = ((lax.rem(sib + 2, 4), sib), (opp, t))
+    w_loads, b_loads, d_loads = {}, {}, {}
+    for c in range(chunks):
+        for h in range(2):
+            for j in range(4):
+                col = pl.multiple_of(owners[h][j % 2] * quarter + c * w, w)
+                ref = gate_ref if j < 2 else up_ref
+                cp = pltpu.make_async_copy(
+                    ref.at[:, pl.ds(col, w)], w_buf.at[c, h, j], load_w.at[c, h, j])
+                cp.start()
+                w_loads[c, h, j] = cp
+                half = fb_ref.shape[1] // 2
+                cb = pltpu.make_async_copy(
+                    fb_ref.at[:, pl.ds((j // 2) * half, half), pl.ds(col, w)],
+                    b_buf.at[c, h, j], load_b.at[c, h, j])
+                cb.start()
+                b_loads[c, h, j] = cb
+    for c in range(chunks):
+        for q, owner in enumerate((t, sib, opp, diag)):
+            row = pl.multiple_of(owner * quarter + c * w, w)
+            cp = pltpu.make_async_copy(
+                down_ref.at[pl.ds(row, w), :], d_buf.at[c, pl.ds(q * w, w), :], load_d.at[c, q])
+            cp.start()
+            d_loads[c, q] = cp
+
+    bar = pltpu.get_barrier_semaphore()
+    pl.semaphore_signal(bar, inc=1, device_id={"tp": sib}, device_id_type=MESH)
+    pl.semaphore_signal(bar, inc=1, device_id={"tp": opp}, device_id_type=MESH)
+    for d in range(1, stores):
+        pl.semaphore_signal(
+            bar, inc=1, device_id={"store": lax.rem(s + d, stores)}, device_id_type=MESH)
+    for u in range(4):
+        @pl.when(jnp.logical_not(jnp.logical_and(s == t, t == u)))
+        def _():
+            pl.semaphore_signal(bar, inc=1, device_id={"store": t, "tp": u}, device_id_type=MESH)
+    meta[s, 0:1, 0:seg_ref.shape[1]] = seg_ref[...]
+    meta[s, 1:2, 0:row_ref.shape[1]] = row_ref[...]
+    pl.semaphore_wait(bar, 2 + (stores - 1) + 4 - jnp.where(s == t, 1, 0))
+
+    meta_copies, tok_copies = [], {}
+    for d in range(1, stores):
+        peer = lax.rem(s + d, stores)
+        cp = remote(meta.at[s], meta.at[s], meta_s.at[d - 1], meta_r.at[d - 1], store=peer)
+        cp.start()
+        meta_copies.append(cp)
+    for r in range(2):
+        n = SPLIT[r]
+        for d in range(1, stores):
+            peer = lax.rem(s + d, stores)
+            cp = remote(
+                tok_ref.at[pl.ds(starts[r], n), :],
+                toks[r].at[pl.ds(pl.multiple_of(s * n, n), n), :],
+                tok_s.at[r, d - 1], tok_r.at[r, d - 1], store=peer)
+            cp.start()
+            tok_copies[r, d] = cp
+        toks[r][pl.ds(pl.multiple_of(s * n, n), n), :] = tok_ref[pl.ds(starts[r], n), :]
+    for cp in meta_copies:
+        cp.wait_recv()
+    pending += meta_copies + list(tok_copies.values())
+
+    per = tok_ref.shape[0]
+    lane = lax.broadcasted_iota(jnp.int32, (per, 128), 1)
+    sub = lax.broadcasted_iota(jnp.int32, (per, 128), 0)
+    slots = slot_ref[...].astype(F32)
+    n_slot = slots.shape[1]
+    lane_slot = lax.broadcasted_iota(jnp.int32, (per, n_slot), 1).astype(F32)
+    lane_f = lane.astype(F32)
+    table = []
+    for g in range(stores):
+        segs = meta[g, 0:1, :].astype(F32)
+        belongs = meta[g, 1:2, :].astype(F32)
+        seg_col = jnp.sum(jnp.where(lane == sub, belongs, 0.0), axis=1, keepdims=True)
+        adp_col = jnp.sum(jnp.where(lane_f == seg_col, segs, 0.0), axis=1, keepdims=True)
+        table.append(jnp.sum(jnp.where(lane_slot == adp_col, slots, 0.0), axis=1, keepdims=True))
+    rows_at = []
+    for r in range(2):
+        n = SPLIT[r]
+        m = n * stores
+        lane_m = lax.broadcasted_iota(jnp.int32, (per, m), 1)
+        sub_m = lax.broadcasted_iota(jnp.int32, (per, m), 0)
+        total = jnp.zeros((1, m), F32)
+        for g in range(stores):
+            hit = lane_m == sub_m - starts[r] + g * n
+            inside = jnp.logical_and(sub_m >= starts[r], sub_m < starts[r] + n)
+            total += jnp.sum(
+                jnp.where(jnp.logical_and(hit, inside), table[g], 0.0), axis=0, keepdims=True)
+        rows_at.append(total)
+
+    rank2 = fa_ref.shape[1]
+    low_copies = {}
+
+    def low_start(r):
+        for d in range(1, stores):
+            tok_copies[r, d].wait_recv()
+        if r == 0:
+            load_a.wait()
+        scores = dot(fa[...].reshape(rows_of * rank2, width), toks[r][...], (1, 1))
+        mine = jnp.zeros((rank2, scores.shape[1]), F32)
+        for a in range(rows_of):
+            here = rows_at[r] == (s * rows_of + a).astype(F32)
+            mine += jnp.where(here, scores[a * rank2:(a + 1) * rank2, :], 0.0)
+        low_sends[r][...] = mine
+        for g in range(stores):
+            cp = remote(
+                low_sends[r], low_recvs[r].at[t], low_s.at[r, g], low_r.at[r, t], store=g, tp=s)
+            own = jnp.logical_and(s == t, s == g)
+            low_copies[r, g] = cp
+
+            @pl.when(jnp.logical_not(own))
+            def _():
+                cp.start()
+
+            @pl.when(own)
+            def _():
+                low_recvs[r][t] = mine
+
+    def low_finish(r):
+        for u in range(4):
+            @pl.when(jnp.logical_not(jnp.logical_and(s == t, t == u)))
+            def _():
+                remote(low_sends[r], low_recvs[r].at[u], low_s.at[r, 0], low_r.at[r, u],
+                       store=t, tp=u).wait_recv()
+        total = low_recvs[r][0] + low_recvs[r][1] + low_recvs[r][2] + low_recvs[r][3]
+        total = total.astype(BF16).astype(F32)
+        half = rank2 // 2
+        for gu in range(2):
+            piece = total[gu * half:(gu + 1) * half, :]
+            placed = jnp.concatenate(
+                [
+                    jnp.where(rows_at[r] == (t * rows_of + a).astype(F32), piece, 0.0)
+                    for a in range(rows_of)
+                ],
+                axis=0,
+            )
+            spreads[r][gu] = placed.T.astype(BF16)
+
+    def term(r, c, h, j):
+        b = b_buf[c, h, j].reshape(spreads[r].shape[2], w)
+        return dot(toks[r][...], w_buf[c, h, j]) + dot(spreads[r][j // 2], b)
+
+    sib_copies, x_copies, hx_copies, h1_copies, h3_copies, z_copies = {}, {}, {}, {}, {}, {}
+
+    def phase1(r, c):
+        if r == 0:
+            for j in range(4):
+                w_loads[c, 0, j].wait()
+                b_loads[c, 0, j].wait()
+
+        @pl.loop(0, 4)
+        def _(j):
+            sib_sends[r][c, j] = term(r, c, 0, j).astype(BF16)
+
+        cp = remote(sib_sends[r].at[c], sib_recvs[r].at[c], sib_s.at[r, c], sib_r.at[r, c], tp=sib)
+        cp.start()
+        sib_copies[r, c] = cp
+        if r == 0:
+            for j in range(4):
+                w_loads[c, 1, j].wait()
+                b_loads[c, 1, j].wait()
+
+        @pl.loop(0, 4)
+        def _(j):
+            keeps[r][c, j] = term(r, c, 1, j)
+
+    def phase2(r, c):
+        sib_copies[r, c].wait_recv()
+        for gu in range(2):
+            x_sends[r][c, gu] = (
+                keeps[r][c, 2 * gu] + sib_recvs[r][c, 2 * gu].astype(F32)).astype(BF16)
+        cp = remote(x_sends[r].at[c], x_recvs[r].at[c], x_s.at[r, c], x_r.at[r, c], tp=opp)
+        cp.start()
+        x_copies[r, c] = cp
+        for gu in range(2):
+            keeps[r][c, 2 * gu + 1] += sib_recvs[r][c, 2 * gu + 1].astype(F32)
+
+    def phase3(r, c):
+        x_copies[r, c].wait_recv()
+        gate = keeps[r][c, 1] + x_recvs[r][c, 0].astype(F32)
+        up = keeps[r][c, 3] + x_recvs[r][c, 1].astype(F32)
+        hids[r][c, :, 0:w] = (gate / (1.0 + jnp.exp(-gate)) * up).astype(BF16)
+        mine = hids[r].at[c, :, pl.ds(0, w)]
+        cp = remote(mine, hids[r].at[c, :, pl.ds(2 * w, w)], hx_s.at[r, c], hx_r.at[r, c], tp=opp)
+        cp.start()
+        hx_copies[r, c] = cp
+        cp = remote(mine, hids[r].at[c, :, pl.ds(w, w)], h1_s.at[r, c], h1_r.at[r, c], tp=sib)
+        cp.start()
+        h1_copies[r, c] = cp
+
+    def phase4(r, c):
+        hx_copies[r, c].wait_recv()
+        cp = remote(
+            hids[r].at[c, :, pl.ds(2 * w, w)], hids[r].at[c, :, pl.ds(3 * w, w)],
+            h3_s.at[r, c], h3_r.at[r, c], tp=sib)
+        cp.start()
+        h3_copies[r, c] = cp
+
+    def phase5(r, c):
+        h1_copies[r, c].wait_recv()
+        h3_copies[r, c].wait_recv()
+        if r == 0:
+            for q in range(4):
+                d_loads[c, q].wait()
+        n = SPLIT[r]
+        tile = 256
+        for lo in range(0, width, tile):
+            value = dot(hids[r][c], d_buf[c, :, lo:lo + tile])
+            if c > 0:
+                value += accs[r][:, lo:lo + tile]
+            if c < chunks - 1:
+                accs[r][:, lo:lo + tile] = value
+            else:
+                z_sends[r][:, lo:lo + tile] = value.astype(BF16)
+        if c == chunks - 1:
+            for d in range(1, stores):
+                peer = lax.rem(s + d, stores)
+                cp = remote(
+                    z_sends[r].at[pl.ds(pl.multiple_of(peer * n, n), n), :],
+                    z_recvs[r].at[d - 1], z_s.at[r, d - 1], z_r.at[r, d - 1], store=peer)
+                cp.start()
+                z_copies[r, d] = cp
+
+    order = [(r, c) for r in range(2) for c in range(chunks)]
+    phases = (phase2, phase3, phase4, phase5)
+    low_start(0)
+    low_finish(0)
+    for k in range(len(order) + LAGS[-1]):
+        if k == 2:
+            low_start(1)
+        if k == chunks:
+            low_finish(1)
+        if k < len(order):
+            phase1(*order[k])
+        for lag, phase in zip(LAGS, phases):
+            if 0 <= k - lag < len(order):
+                phase(*order[k - lag])
+    for r in range(2):
+        n = SPLIT[r]
+        total = z_sends[r][pl.ds(pl.multiple_of(s * n, n), n), :].astype(F32)
+        for d in range(1, stores):
+            z_copies[r, d].wait_recv()
+            total += z_recvs[r][d - 1].astype(F32)
+        out_ref[starts[r]:starts[r] + n, :] = total.astype(BF16)
+    for group in (sib_copies, x_copies, hx_copies, h1_copies, h3_copies, z_copies):
+        pending += list(group.values())
+    for cp in pending:
+        cp.wait_send()
+    for (r, g), cp in low_copies.items():
+        @pl.when(jnp.logical_not(jnp.logical_and(s == t, s == g)))
+        def _():
+            cp.wait_send()
+
+
+def fused_body(
+    tokens, gate_weight, up_weight, down_weight, factor_a, factor_b,
+    adapter_slot, seg_adapter, row_segment,
+):
+    stores = lax.axis_size("store")
+    ff_loc, width = down_weight.shape
+    w = CHUNK
+    chunks = ff_loc // 4 // w
+    rows_of, rank2, _ = factor_a.shape
+    half = rank2 // 2
+    m = tuple(n * stores for n in SPLIT)
+
+    def both(shape_of, kind):
+        return [pltpu.VMEM(shape_of(r), kind) for r in range(2)]
+
+    dma = pltpu.SemaphoreType.DMA
+    scratch = [
+        pltpu.VMEM((stores, 8, 128), jnp.int32),
+        *both(lambda r: (m[r], width), BF16),
+        pltpu.VMEM(factor_a.shape, BF16),
+        pltpu.VMEM((chunks, 2, 4, width, w), BF16),
+        pltpu.VMEM((chunks, 2, 4, rows_of, half, w), BF16),
+        pltpu.VMEM((chunks, 4 * w, width), BF16),
+        *both(lambda r: (rank2, m[r]), F32),
+        *both(lambda r: (4, rank2, m[r]), F32),
+        *both(lambda r: (2, m[r], rows_of * half), BF16),
+        *both(lambda r: (chunks, 4, m[r], w), BF16),
+        *both(lambda r: (chunks, 4, m[r], w), BF16),
+        *both(lambda r: (chunks, 4, m[r], w), F32),
+        *both(lambda r: (chunks, 2, m[r], w), BF16),
+        *both(lambda r: (chunks, 2, m[r], w), BF16),
+        *both(lambda r: (chunks, m[r], 4 * w), BF16),
+        *both(lambda r: (m[r], width), F32),
+        *both(lambda r: (m[r], width), BF16),
+        *both(lambda r: (stores - 1, SPLIT[r], width), BF16),
+        dma((chunks, 2, 4)), dma((chunks, 2, 4)), dma((chunks, 4)), dma,
+        dma((stores - 1,)), dma((stores - 1,)),
+        dma((2, stores - 1)), dma((2, stores - 1)),
+        dma((2, stores)), dma((2, 4)),
+        *[dma((2, chunks)) for _ in range(10)],
+        dma((2, stores - 1)), dma((2, stores - 1)),
+    ]
+    vmem = pl.BlockSpec(memory_space=pltpu.VMEM)
+    hbm = pl.BlockSpec(memory_space=pl.ANY)
+    return pl.pallas_call(
+        fused_kernel,
+        out_shape=jax.ShapeDtypeStruct(tokens.shape, BF16),
+        in_specs=[vmem, hbm, hbm, hbm, hbm, hbm, vmem, vmem, vmem],
+        out_specs=vmem,
+        scratch_shapes=scratch,
+        compiler_params=pltpu.CompilerParams(
+            collective_id=0, has_side_effects=True, vmem_limit_bytes=60 * 1024 * 1024
+        ),
+    )(
+        tokens, gate_weight, up_weight, down_weight, factor_a, factor_b,
+        adapter_slot.reshape(1, -1), seg_adapter, row_segment,
+    )
+
+
 def solution(mesh):
     placed = (
         P(("rep", "store"), "tp"),
@@ -115,6 +481,7 @@
         P(("rep", "store"), None),
         P(("rep", "store"), None),
     )
+    fused = mesh.shape["store"] == 4 and mesh.shape["tp"] == 4
     return jax.shard_map(
-        body, mesh=mesh, in_specs=placed, out_specs=P(("rep", "store"), "tp"), check_vma=False
-    )
+        fused_body if fused else body, mesh=mesh, in_specs=placed, out_specs=P(("rep", "store"), "tp"), check_vma=False
+    )

time: 240 us -> 68.1 us (0.28)
  blocking collectives: 95.7 us -> 0 us
  waiting for transfers between devices: 91.7 us -> 0 us
  Pallas kernels: 0 us -> 66.4 us
  matrix products: 27.3 us -> 0 us
  between operations: 13.6 us -> 0.01 us
  starting transfers between devices: 4.65 us -> 0 us
  other arithmetic: 3.1 us -> 0 us
  local copies, waits for them, and re-layouts: 4.23 us -> 1.56 us
    all_gather x4 -> x0, blocking collectives: 85.6 us -> none  [the longest x1 35.8 us: body(): lax.all_gather(row_segment, 'store', axis=0, tiled=True)]
    psum x1 -> x0, waiting for transfers between devices: 70.1 us -> none  [body(): lax.psum(up_part.astype(jnp.bfloat16), 'tp').astype(jnp.float32)]
    pallas_call x0 -> x1, Pallas kernels: none -> 66.4 us  [fused_body(): pl.pallas_call(fused_kernel, out_shape=jax.ShapeDtypeStruct(tokens.shape,...]
    dot_general x6 -> x0, matrix products: 27.3 us -> none  [the longest x1 8.46 us: body(): jnp.dot(hidden, down_weight, preferred_element_type=jnp.float32)]
    reduce_scatter x1 -> x0, waiting for transfers between devices: 21.6 us -> none  [body(): lax.psum_scatter(jnp.dot(hidden, down_weight, preferred_element_type=jnp....]
    psum x1 -> x0, blocking collectives: 10.1 us -> none  [body(): home_low = lax.psum(partial_value, 'tp')]
    all_to_all x1 -> x0, starting transfers between devices: 4.57 us -> none  [body(): lax.all_to_all(blocks, 'store', split_axis=0, concat_axis=0, tiled=True)]
    gather x2 -> x0, local copies, waits for them, and re-layouts: 2.89 us -> none  [the longest x1 2.22 us: body(): jnp.take(received.reshape(store_count * capacity, rank_both, d_loc), pick...]
  transfers between devices with their start and end apart: 3 -> 0, of which waited for: 2 -> 0; matrix products, arithmetic and copies ran while one was open for 5% -> 0% of each run, Pallas kernels for 0% -> 0%
where the time goes in v1:
time: 68.1 us; the launch traced here: 68 us
  Pallas kernels  66.4 us (98%)
  local copies, waits for them, and re-layouts  1.56 us (2%)
    pallas_call x1, Pallas kernels, fused_body(): pl.pallas_call(fused_kernel, out_shape=jax.ShapeDtypeStruct(tokens.shape,...  66.4 us
    unnamed x1, local copies, waits for them, and re-layouts  1.56 us

profile of v1, /device:TPU:0, one launch (start us, length us, event | category | flops | bytes accessed | tf_op | source)
XLA Modules:
  0.0 68.0 jit_solution(16797302519439698555)
XLA Ops:
  0.0 66.4 %shard_map.91 = bf16[48,1280]{1,0:T(8,128)(2,1)} custom-call(bf16[48,1280]{1,0:T(8,128)(2,1)} %tok_ref.1, bf16[1280,4096]{1,0:T(8,128)(2,1)} %gate_ref.1, bf16[1280,4096]{1,0:T(8,128)(2,1)} %up_ref.1, bf16[4096,1280]{1,0:T(8,128)(2,1)} %down_ref.1, bf16[16,32,1280]{2,1,0:T(8,128)(2,1)} %fa_ref.1, bf16[16,32,4096]{2,1,0:T(8,128)(2,1)} %fb_ref.1, ...), custom_call_target="tpu_custom_call" | custom-call | tf_op jit(solution)/shard_map/pallas_call | solution.py:457
  66.4 1.6 %copy.11 = bf16[48,1280]{1,0:T(8,128)(2,1)} copy(bf16[48,1280]{1,0:T(8,128)(2,1)} %shard_map.91) | data formatting | bytes 245760

commit v2 on v1

--- a/solution.py
+++ b/solution.py
@@ -9,7 +9,8 @@
 MESH = pl.DeviceIdType.MESH
 CHUNK = 256
 SPLIT = (32, 16)
-LAGS = (1, 2, 3, 4)
+LAGS = (1, 3, 5, 6)
+EARLY = 1
 F32 = jnp.float32
 BF16 = jnp.bfloat16
 
@@ -121,11 +122,8 @@
 def fused_kernel(
     tok_ref, gate_ref, up_ref, down_ref, fa_ref, fb_ref, slot_ref, seg_ref, row_ref,
     out_ref,
-    meta, tok_a, tok_b, fa, w_buf, b_buf, d_buf,
-    low_send_a, low_send_b, low_recv_a, low_recv_b, spread_a, spread_b,
-    sib_send_a, sib_send_b, sib_recv_a, sib_recv_b, keep_a, keep_b,
-    x_send_a, x_send_b, x_recv_a, x_recv_b, hid_a, hid_b, acc_a, acc_b,
-    z_send_a, z_send_b, z_recv_a, z_recv_b,
+    meta, toks, fa, w_buf, b_buf, d_buf, low_sends, low_recvs, spreads,
+    sib_sends, sib_recvs, keeps, x_sends, x_recvs, hids, accs, z_sends, z_recvs,
     load_w, load_b, load_d, load_fa,
     meta_s, meta_r, tok_s, tok_r, low_s, low_r, sib_s, sib_r, x_s, x_r,
     hx_s, hx_r, h1_s, h1_r, h3_s, h3_r, z_s, z_r,
@@ -142,12 +140,8 @@
     quarter = ff_loc // 4
     w = CHUNK
     chunks = quarter // w
-    toks, low_sends, low_recvs = (tok_a, tok_b), (low_send_a, low_send_b), (low_recv_a, low_recv_b)
-    spreads = (spread_a, spread_b)
-    sib_sends, sib_recvs, keeps = (sib_send_a, sib_send_b), (sib_recv_a, sib_recv_b), (keep_a, keep_b)
-    x_sends, x_recvs, hids, accs = (x_send_a, x_send_b), (x_recv_a, x_recv_b), (hid_a, hid_b), (acc_a, acc_b)
-    z_sends, z_recvs = (z_send_a, z_send_b), (z_recv_a, z_recv_b)
-    starts = (0, SPLIT[0])
+    blocks = len(SPLIT)
+    starts = tuple(sum(SPLIT[:r]) for r in range(blocks))
     pending = []
 
     def remote(src, dst, send_sem, recv_sem, **where):
@@ -160,7 +154,9 @@
     load_a.start()
     owners = ((lax.rem(sib + 2, 4), sib), (opp, t))
     w_loads, b_loads, d_loads = {}, {}, {}
-    for c in range(chunks):
+
+    def load_columns(c):
+        half = fb_ref.shape[1] // 2
         for h in range(2):
             for j in range(4):
                 col = pl.multiple_of(owners[h][j % 2] * quarter + c * w, w)
@@ -169,19 +165,22 @@
                     ref.at[:, pl.ds(col, w)], w_buf.at[c, h, j], load_w.at[c, h, j])
                 cp.start()
                 w_loads[c, h, j] = cp
-                half = fb_ref.shape[1] // 2
                 cb = pltpu.make_async_copy(
                     fb_ref.at[:, pl.ds((j // 2) * half, half), pl.ds(col, w)],
                     b_buf.at[c, h, j], load_b.at[c, h, j])
                 cb.start()
                 b_loads[c, h, j] = cb
-    for c in range(chunks):
+
+    def load_down(c):
         for q, owner in enumerate((t, sib, opp, diag)):
             row = pl.multiple_of(owner * quarter + c * w, w)
             cp = pltpu.make_async_copy(
                 down_ref.at[pl.ds(row, w), :], d_buf.at[c, pl.ds(q * w, w), :], load_d.at[c, q])
             cp.start()
             d_loads[c, q] = cp
+
+    for c in range(EARLY):
+        load_columns(c)
 
     bar = pltpu.get_barrier_semaphore()
     pl.semaphore_signal(bar, inc=1, device_id={"tp": sib}, device_id_type=MESH)
@@ -203,7 +202,7 @@
         cp = remote(meta.at[s], meta.at[s], meta_s.at[d - 1], meta_r.at[d - 1], store=peer)
         cp.start()
         meta_copies.append(cp)
-    for r in range(2):
+    for r in range(blocks):
         n = SPLIT[r]
         for d in range(1, stores):
             peer = lax.rem(s + d, stores)
@@ -214,6 +213,10 @@
             cp.start()
             tok_copies[r, d] = cp
         toks[r][pl.ds(pl.multiple_of(s * n, n), n), :] = tok_ref[pl.ds(starts[r], n), :]
+    for c in range(EARLY, chunks):
+        load_columns(c)
+    for c in range(chunks):
+        load_down(c)
     for cp in meta_copies:
         cp.wait_recv()
     pending += meta_copies + list(tok_copies.values())
@@ -233,7 +236,7 @@
         adp_col = jnp.sum(jnp.where(lane_f == seg_col, segs, 0.0), axis=1, keepdims=True)
         table.append(jnp.sum(jnp.where(lane_slot == adp_col, slots, 0.0), axis=1, keepdims=True))
     rows_at = []
-    for r in range(2):
+    for r in range(blocks):
         n = SPLIT[r]
         m = n * stores
         lane_m = lax.broadcasted_iota(jnp.int32, (per, m), 1)
@@ -379,21 +382,22 @@
                 cp.start()
                 z_copies[r, d] = cp
 
-    order = [(r, c) for r in range(2) for c in range(chunks)]
+    order = [(r, c) for r in range(blocks) for c in range(chunks)]
     phases = (phase2, phase3, phase4, phase5)
     low_start(0)
     low_finish(0)
     for k in range(len(order) + LAGS[-1]):
-        if k == 2:
-            low_start(1)
-        if k == chunks:
-            low_finish(1)
+        for r in range(1, blocks):
+            if k == r * chunks - 2:
+                low_start(r)
+            if k == r * chunks:
+                low_finish(r)
         if k < len(order):
             phase1(*order[k])
         for lag, phase in zip(LAGS, phases):
             if 0 <= k - lag < len(order):
                 phase(*order[k - lag])
-    for r in range(2):
+    for r in range(blocks):
         n = SPLIT[r]
         total = z_sends[r][pl.ds(pl.multiple_of(s * n, n), n), :].astype(F32)
         for d in range(1, stores):
@@ -422,35 +426,37 @@
     half = rank2 // 2
     m = tuple(n * stores for n in SPLIT)
 
-    def both(shape_of, kind):
-        return [pltpu.VMEM(shape_of(r), kind) for r in range(2)]
+    blocks = len(SPLIT)
+
+    def each(shape_of, kind):
+        return [pltpu.VMEM(shape_of(r), kind) for r in range(blocks)]
 
     dma = pltpu.SemaphoreType.DMA
     scratch = [
         pltpu.VMEM((stores, 8, 128), jnp.int32),
-        *both(lambda r: (m[r], width), BF16),
+        each(lambda r: (m[r], width), BF16),
         pltpu.VMEM(factor_a.shape, BF16),
         pltpu.VMEM((chunks, 2, 4, width, w), BF16),
         pltpu.VMEM((chunks, 2, 4, rows_of, half, w), BF16),
         pltpu.VMEM((chunks, 4 * w, width), BF16),
-        *both(lambda r: (rank2, m[r]), F32),
-        *both(lambda r: (4, rank2, m[r]), F32),
-        *both(lambda r: (2, m[r], rows_of * half), BF16),
-        *both(lambda r: (chunks, 4, m[r], w), BF16),
-        *both(lambda r: (chunks, 4, m[r], w), BF16),
-        *both(lambda r: (chunks, 4, m[r], w), F32),
-        *both(lambda r: (chunks, 2, m[r], w), BF16),
-        *both(lambda r: (chunks, 2, m[r], w), BF16),
-        *both(lambda r: (chunks, m[r], 4 * w), BF16),
-        *both(lambda r: (m[r], width), F32),
-        *both(lambda r: (m[r], width), BF16),
-        *both(lambda r: (stores - 1, SPLIT[r], width), BF16),
+        each(lambda r: (rank2, m[r]), F32),
+        each(lambda r: (4, rank2, m[r]), F32),
+        each(lambda r: (2, m[r], rows_of * half), BF16),
+        each(lambda r: (chunks, 4, m[r], w), BF16),
+        each(lambda r: (chunks, 4, m[r], w), BF16),
+        each(lambda r: (chunks, 4, m[r], w), F32),
+        each(lambda r: (chunks, 2, m[r], w), BF16),
+        each(lambda r: (chunks, 2, m[r], w), BF16),
+        each(lambda r: (chunks, m[r], 4 * w), BF16),
+        each(lambda r: (m[r], width), F32),
+        each(lambda r: (m[r], width), BF16),
+        each(lambda r: (stores - 1, SPLIT[r], width), BF16),
         dma((chunks, 2, 4)), dma((chunks, 2, 4)), dma((chunks, 4)), dma,
         dma((stores - 1,)), dma((stores - 1,)),
-        dma((2, stores - 1)), dma((2, stores - 1)),
-        dma((2, stores)), dma((2, 4)),
-        *[dma((2, chunks)) for _ in range(10)],
-        dma((2, stores - 1)), dma((2, stores - 1)),
+        dma((blocks, stores - 1)), dma((blocks, stores - 1)),
+        dma((blocks, stores)), dma((blocks, 4)),
+        *[dma((blocks, chunks)) for _ in range(10)],
+        dma((blocks, stores - 1)), dma((blocks, stores - 1)),
     ]
     vmem = pl.BlockSpec(memory_space=pltpu.VMEM)
     hbm = pl.BlockSpec(memory_space=pl.ANY)

time: 68.1 us -> 65.6 us (0.963)
  Pallas kernels: 66.4 us -> 63.8 us
    pallas_call x1, Pallas kernels: 66.4 us -> 63.8 us  [fused_body(): pl.pallas_call(fused_kernel, out_shape=jax.ShapeDtypeStruct(tokens.shape,...]
where the time goes in v2:
time: 65.6 us; the launch traced here: 65.4 us
  Pallas kernels  63.8 us (97%)
  local copies, waits for them, and re-layouts  1.56 us (2%)
    pallas_call x1, Pallas kernels, fused_body(): pl.pallas_call(fused_kernel, out_shape=jax.ShapeDtypeStruct(tokens.shape,...  63.8 us
    unnamed x1, local copies, waits for them, and re-layouts  1.56 us

profile of v2, /device:TPU:0, one launch (start us, length us, event | category | flops | bytes accessed | tf_op | source)
XLA Modules:
  0.0 65.4 jit_solution(2084809279489730471)
XLA Ops:
  0.0 63.8 %shard_map.91 = bf16[48,1280]{1,0:T(8,128)(2,1)} custom-call(bf16[48,1280]{1,0:T(8,128)(2,1)} %tok_ref.1, bf16[1280,4096]{1,0:T(8,128)(2,1)} %gate_ref.1, bf16[1280,4096]{1,0:T(8,128)(2,1)} %up_ref.1, bf16[4096,1280]{1,0:T(8,128)(2,1)} %down_ref.1, bf16[16,32,1280]{2,1,0:T(8,128)(2,1)} %fa_ref.1, bf16[16,32,4096]{2,1,0:T(8,128)(2,1)} %fb_ref.1, ...), custom_call_target="tpu_custom_call" | custom-call | tf_op jit(solution)/shard_map/pallas_call | solution.py:463
  63.8 1.6 %copy.11 = bf16[48,1280]{1,0:T(8,128)(2,1)} copy(bf16[48,1280]{1,0:T(8,128)(2,1)} %shard_map.91) | data formatting | bytes 245760
